TPU v7x, 32 devices: a whole 2x2x4 slice. The times are simulated.
32 devices in a mesh: groups: 1, pool: 32 (over z, y, x, core), tensor: 1.
Axes of the slice: x: 2, y: 2, z: 4, core: 2. Of those that a mesh axis runs over, the one named last changes fastest.
Arguments:
- hidden_input: bfloat16 [256, 8192], P(('groups', 'pool')), may hold values from -6 to 6
- key_value_weight: bfloat16 [8192, 2048], P('pool', 'tensor'), may hold values from -0.0625 to 0.0625
- adapter_down_weight: bfloat16 [32, 64, 8192], P('groups', 'tensor', 'pool'), may hold values from -0.0625 to 0.0625
- adapter_up_weight: bfloat16 [32, 64, 2048], P(('groups', 'pool'), None, 'tensor'), may hold values from -0.75 to 0.75
- adapter_of_row: int32 [256, 1], P('groups'), may hold values from 0 to 31
- adapter_page_table: int32 [32], P('groups'), may hold values from 0 to 31, each once
- cached_length: int32 [256], P(('groups', 'pool')), may hold values from 2 to 512, as said below
- queries: bfloat16 [256, 8192], P(('groups', 'pool'), 'tensor'), may hold values from -100 to 100
- key_value_cache: bfloat16 [256, 512, 2048], P(('groups', 'pool'), None, 'tensor'), may hold values from -4.5 to 4.5
Outputs:
- fresh_key_value: bfloat16 [256, 2048], P(('groups', 'pool'), 'tensor')
- attended: bfloat16 [256, 8192], P(('groups', 'pool'), 'tensor')
Inputs may be any that keep to these rules, and one draw needn't show every extreme that they name: adapter_page_table[a] is the page of adapter a; pool index p holds page p. `adapter_of_row`: every adapter is used by some row. `cached_length`: some row of every replica holds the full 512.
All inputs are finite; a program needn't handle non-finite values.
Results may differ from a plain program's by a relative error of at most 0.0049.
Values may be sent and summed in bfloat16 or wider, within the bound.
A program may use at most 128 MiB of HBM per device.

v0:
```python
import math

import jax
import jax.numpy as jnp
from jax import lax
from jax.sharding import PartitionSpec as P

QH = 64
KVH = 8
HD = 128


ADAPTER_SCALE = 0.5


def attend_rows(query_block, stored, new_kv, lengths):
    inv_root = 1.0 / math.sqrt(query_block.shape[-1])
    cache_keys = stored[:, :, :, 0, :]
    cache_vals = stored[:, :, :, 1, :]
    scores = (
        jnp.einsum("rkgd,rlkd->rkgl", query_block, cache_keys, preferred_element_type=jnp.float32)
        * inv_root
    )
    own_score = (
        jnp.einsum(
            "rkgd,rkd->rkg", query_block, new_kv[:, :, 0, :], preferred_element_type=jnp.float32
        )
        * inv_root
    )
    positions = jnp.arange(stored.shape[1])
    in_cache = positions[None, None, None, :] < lengths[:, None, None, None]
    scores = jnp.where(in_cache, scores, -jnp.inf)
    peak = jnp.maximum(jnp.max(scores, axis=-1), own_score)
    weights = jnp.exp(scores - peak[..., None])
    own_weight = jnp.exp(own_score - peak)
    weight_sum = jnp.sum(weights, axis=-1) + own_weight
    weights_b = weights.astype(jnp.bfloat16)
    own_b = own_weight.astype(jnp.bfloat16)
    mixture = jnp.einsum(
        "rkgl,rlkd->rkgd", weights_b, cache_vals, preferred_element_type=jnp.float32
    )
    new_vals = new_kv[:, :, 1, :].astype(jnp.float32)
    mixture = mixture + own_b.astype(jnp.float32)[..., None] * new_vals[:, :, None, :]
    return (mixture / weight_sum[..., None]).astype(jnp.bfloat16)


def body(
    hidden_input,
    key_value_weight,
    adapter_down_weight,
    adapter_up_weight,
    adapter_of_row,
    adapter_page_table,
    cached_length,
    queries,
    key_value_cache,
):
    local_rows = hidden_input.shape[0]
    pool_index = lax.axis_index("pool")
    adapter_list = adapter_of_row[:, 0]
    slices = lax.all_to_all(hidden_input, "pool", split_axis=1, concat_axis=0, tiled=True)
    rows_in = slices
    base_output = lax.psum_scatter(
        jnp.dot(rows_in, key_value_weight, preferred_element_type=jnp.float32),
        "pool",
        scatter_dimension=0,
        tiled=True,
    )
    rows_in = slices
    selected_down = jnp.take(adapter_down_weight, adapter_list, axis=0)
    shrink_part = lax.psum_scatter(
        jnp.einsum("rd,rkd->rk", rows_in, selected_down, preferred_element_type=jnp.float32),
        "pool",
        scatter_dimension=0,
        tiled=True,
    )
    rank_half = shrink_part.astype(jnp.bfloat16)
    rank_full = lax.all_gather(rank_half, "tensor", axis=1, tiled=True)
    local_ids = lax.dynamic_slice_in_dim(adapter_list, pool_index * local_rows, local_rows, 0)
    slot_ids = jnp.take(adapter_page_table, local_ids)
    paged_up_block = lax.all_gather(adapter_up_weight, "pool", axis=0, tiled=True)
    inside = (slot_ids >= 0) & (slot_ids < paged_up_block.shape[0])
    selected_down = jnp.take(
        paged_up_block, jnp.clip(slot_ids, 0, paged_up_block.shape[0] - 1), axis=0
    )
    product = jnp.einsum("rk,rkc->rc", rank_full, selected_down, preferred_element_type=jnp.float32)
    adapter_delta = jnp.where(inside[:, None], product, 0.0)
    fresh_key_value = (base_output + ADAPTER_SCALE * adapter_delta).astype(jnp.bfloat16)
    group_size = QH // KVH
    local_heads = queries.shape[1] // (group_size * HD)
    query_block = queries.reshape(local_rows, local_heads, group_size, HD)
    stored = key_value_cache.reshape(local_rows, key_value_cache.shape[1], local_heads, 2, HD)
    new_kv = fresh_key_value.reshape(local_rows, local_heads, 2, HD)
    attended = attend_rows(query_block, stored, new_kv, cached_length).reshape(
        local_rows, queries.shape[1]
    )
    return (fresh_key_value, attended)


def solution(mesh):
    in_specs = (
        P(("groups", "pool"), None),
        P("pool", "tensor"),
        P("groups", "tensor", "pool"),
        P(("groups", "pool"), None, "tensor"),
        P("groups", None),
        P("groups"),
        P(("groups", "pool")),
        P(("groups", "pool"), "tensor"),
        P(("groups", "pool"), None, "tensor"),
    )
    out_specs = (P(("groups", "pool"), "tensor"), P(("groups", "pool"), "tensor"))
    return jax.shard_map(body, mesh=mesh, in_specs=in_specs, out_specs=out_specs, check_vma=False)
```

profile of v0, /device:TPU:0, one launch (start us, length us, event | category | flops | bytes accessed | tf_op | source)
XLA Modules:
  0.0 244.9 jit_solution(10124932819853142984)
XLA Ops:
  7.2 0.0 copy-start
  7.2 0.0 all-gather.2.cloned.1.call-start
  7.2 0.7 all-gather.2.cloned.1.call-update
  7.9 0.0 reduce-scatter.2.cloned.1.call-start
  8.0 15.5 %all_to_all.19 = bf16[8,32,256]{2,0,1:T(8,128)(2,1)S(1)} all-to-all(bf16[8,32,256]{2,0,1:T(8,128)(2,1)} %bitcast.83), channel_id=1, replica_groups=mesh['groups'=1,'pool'=32,'tensor'=1] {'pool'}, dimensions={1} | all-to-all | bytes 262144 | tf_op jit(solution)/shard_map/all_to_all | solution.py:61
  23.5 3.0 %fusion.21 = f32[256,2048]{1,0:T(8,128)} fusion(bf16[256,2048]{1,0:T(8,128)(2,1)} %param.10, bf16[8,32,256]{2,0,1:T(8,128)(2,1)S(1)} %all_to_all.19), kind=kOutput, calls=%fused_computation.27 | convolution fusion | flops 268435456 | bytes 3276800 | tf_op jit(solution)/shard_map/dot_general | solution.py:64
  26.5 0.0 reduce-scatter.2.cloned.1.call-update
  26.5 0.0 copy-start.5
  26.5 0.0 copy-start.1
  26.6 21.7 %copy.18 = bf16[8,512,2048]{1,2,0:T(8,128)(2,1)} copy(bf16[8,512,2048]{2,1,0:T(8,128)(2,1)} %param.17) | data formatting | bytes 33554432 | tf_op args[8]
  48.3 0.0 copy-done.5
  48.3 0.1 fusion.37
  48.4 0.0 copy-done.1
  48.4 0.6 gather_fusion
  49.1 0.0 copy-done
  49.1 0.0 copy-start.6
  49.1 0.0 copy-start.3
  49.1 8.6 %gather_fusion.1 = bf16[256,64,256]{2,1,0:T(8,128)(2,1)} fusion(bf16[32,64,256]{2,1,0:T(8,128)(2,1)S(1)} %copy-done, s32[1024]{0:T(1024)S(1)} %pad_clamp_fusion.1), kind=kCustom, calls=%fused_computation.1 | custom fusion | bytes 16778240 | tf_op jit(solution)/shard_map/jit(_take)/gather | solution.py:70
  57.7 0.1 and_bitcast_fusion.1
  57.8 0.0 copy-done.6
  57.8 0.1 iota_compare_fusion
  57.9 0.0 copy-done.3
  57.9 0.0 copy-start.2
  57.9 4.8 %fusion.38 = (f32[8,8,8]{2,1,0:T(8,128)S(1)}, f32[8,8,8,512]{3,2,1,0:T(8,128)S(1)}) fusion(bf16[8,512,8,2,128]{1,4,3,2,0:T(8,128)(2,1)} %bitcast.74, bf16[8,8,8,128]{3,0,2,1:T(8,128)(2,1)S(1)} %bitcast.77, pred[8,512]{1,0:T(8,128)(4,1)S(1)} %iota_compare_fusion), kind=kOutput, calls=%fused_computation.62 | convolution fusion | flops 67894784 | bytes 9574400 | tf_op jit(solution)/shard_map/rkgd,rlkd->rkgl/dot_general | solution.py:21
  62.7 2.1 copy-done.2
  64.8 2.5 %fusion.2 = f32[256,1,64]{2,1,0:T(1,128)S(1)} fusion(bf16[256,64,256]{2,1,0:T(8,128)(2,1)S(1)} %copy-done.2, pred[256]{0:T(512)(128)(4,1)S(1)} %get-tuple-element.4, bf16[256,256,1]{1,0,2:T(8,128)(2,1)S(1)} %bitcast.76), kind=kOutput, calls=%fused_computation.7 | convolution fusion | flops 12582912 | bytes 8585472 | tf_op jit(solution)/shard_map/rd,rkd->rk/dot_general | solution.py:72
  67.3 40.1 %all-reduce = bf16[256,64]{1,0:T(8,128)(2,1)S(1)} all-reduce(f32[256,64]{1,0:T(8,128)S(1)} %bitcast.82), channel_id=3, replica_groups=mesh['groups'=1,'pool'=32,'tensor'=1] {'pool'}, use_global_device_ids=true, to_apply=%region_1.2.clone | all-reduce | flops 16384 | bytes 98304
  107.4 0.0 all-gather.2.cloned.1.call-done
  107.5 5.4 %gather_fusion.2 = bf16[8,64,2048]{2,1,0:T(8,128)(2,1)} fusion(bf16[32,64,2048]{2,1,0:T(8,128)(2,1)} %all-gather.2.cloned.1.call-done, s32[1024]{0:T(1024)S(1)} %pad_clamp_fusion), kind=kCustom, calls=%fused_computation.2 | custom fusion | bytes 4194336 | tf_op jit(solution)/shard_map/jit(_take)/gather | solution.py:83
  112.9 2.0 fusion.6
  115.0 115.1 %reduce-scatter.2.cloned.1.call-done = f32[8,2048]{1,0:T(8,128)} async-done(((f32[256,2048]{1,0:T(8,128)}), f32[8,2048]{1,0:T(8,128)}) %reduce-scatter.2.cloned.1.call-update) | async-done | bytes 65552 | tf_op jit(solution)/shard_map/reduce_scatter | solution.py:63
  230.1 0.9 fusion.28
  231.0 0.0 copy-start.4
  231.0 0.2 fusion.23
  231.2 0.4 fusion.16
  231.6 5.7 %fusion.14 = bf16[1,8,64,128]{3,2,1,0:T(8,128)(2,1)S(1)} fusion(bf16[8,512,8,2,128]{1,4,3,2,0:T(8,128)(2,1)} %bitcast.75, f32[8,8,8,512]{3,2,1,0:T(8,128)S(1)} %get-tuple-element.11, f32[8,8,8]{2,1,0:T(8,128)S(1)} %multiply_maximum_fusion, f32[8,8,8]{2,1,0:T(8,128)S(1)} %get-tuple-element.7, f32[8,8,128]{2,1,0:T(8,128)S(1)} %copy.22, ...), kind=kOutput, calls=%fused_computation.19 | convolution fusion | flops 67895296 | bytes 9607168 | tf_op jit(solution)/shard_map/rkgl,rlkd->rkgd/dot_general | solution.py:39
  237.3 0.8 copy.46
  238.1 0.0 copy-done.4
  (11 shorter events, 0.1 us)
Async XLA Ops:
  7.2 41.9 %copy-start = (bf16[32,64,256]{2,1,0:T(8,128)(2,1)S(1)}, bf16[32,64,256]{2,1,0:T(8,128)(2,1)}, u32[]{:S(2)}) copy-start(bf16[32,64,256]{2,1,0:T(8,128)(2,1)} %param.11) | copy-start | bytes 3145732
  7.2 100.3 %all-gather.2.cloned.1.call-start = ((), (), s32[]{:S(2)}) async-start(), calls=%async_computation.3 | async-start | bytes 8650752 | tf_op jit(solution)/shard_map/all_gather | solution.py:81
  7.9 222.1 %reduce-scatter.2.cloned.1.call-start = ((), (), s32[]{:S(2)}) async-start(), calls=%async_computation.2 | async-start | bytes 2162688 | tf_op jit(solution)/shard_map/reduce_scatter | solution.py:63
  26.5 21.8 %copy-start.5 = (s32[256,1]{0,1:T(1,128)S(1)}, s32[256,1]{0,1:T(1,128)}, u32[]{:S(2)}) copy-start(s32[256,1]{0,1:T(1,128)} %param.13) | copy-start | bytes 3076
  26.5 21.8 %copy-start.1 = (s32[32]{0:T(128)S(1)}, s32[32]{0:T(128)}, u32[]{:S(2)}) copy-start(s32[32]{0:T(128)} %param.14) | copy-start | bytes 388
  49.1 8.7 %copy-start.6 = (s32[8]{0:T(128)S(1)}, s32[8]{0:T(128)}, u32[]{:S(2)}) copy-start(s32[8]{0:T(128)} %param.15) | copy-start | bytes 100
  49.1 8.8 %copy-start.3 = (bf16[8,8192]{1,0:T(8,128)(2,1)S(1)}, bf16[8,8192]{1,0:T(8,128)(2,1)}, u32[]{:S(2)}) copy-start(bf16[8,8192]{1,0:T(8,128)(2,1)} %param.16) | copy-start | bytes 393220
  57.9 6.9 %copy-start.2 = (bf16[256,64,256]{2,1,0:T(8,128)(2,1)S(1)}, bf16[256,64,256]{2,1,0:T(8,128)(2,1)}, u32[]{:S(2)}) copy-start(bf16[256,64,256]{2,1,0:T(8,128)(2,1)} %gather_fusion.1) | copy-start | bytes 25165828
  231.0 7.1 %copy-start.4 = (bf16[8,2048]{1,0:T(8,128)(2,1)}, bf16[8,2048]{1,0:T(8,128)(2,1)S(1)}, u32[]{:S(2)}) copy-start(bf16[8,2048]{1,0:T(8,128)(2,1)S(1)} %fusion.28) | copy-start | bytes 98308
Sparse Core Ops, SparseCore 0:
  10.9 81.1 all-gather.1
  94.3 135.7 reduce-scatter.1
where the time goes:
time: 246 us; the launch traced here: 245 us
  waiting for transfers between devices  116 us (47%)
  blocking collectives  55.6 us (23%)
  local copies, waits for them, and re-layouts  39.3 us (16%)
  matrix products  18.3 us (7%)
  between operations  14.2 us (6%)
    reduce_scatter x1, waiting for transfers between devices, body(): lax.psum_scatter(jnp.dot(rows_in, key_value_weight, preferred_element_typ...  115 us
    unnamed x1, blocking collectives  40.1 us
    unnamed x16, local copies, waits for them, and re-layouts  24.6 us
    all_to_all x1, blocking collectives, body(): lax.all_to_all(hidden_input, 'pool', split_axis=1, concat_axis=0, tiled=T...  15.5 us
    gather x1, local copies, waits for them, and re-layouts, body(): selected_down = jnp.take(adapter_down_weight, adapter_list, axis=0)  8.58 us
    dot_general x1, matrix products, attend_rows(): jnp.einsum('rkgl,rlkd->rkgd', weights_b, cache_vals, preferred_element_ty...  5.7 us
    gather x1, local copies, waits for them, and re-layouts, body(): jnp.take(paged_up_block, jnp.clip(slot_ids, 0, paged_up_block.shape[0] -...  5.44 us
  transfers between devices with their start and end apart: 2, of which 1 were waited for; matrix products, arithmetic and copies ran while one was open for 20% of the time, Pallas kernels for 0%

commit v1 on v0

v1 whole, which is shorter than its diff:
```python
import functools
import math

import jax
import jax.numpy as jnp
from jax import lax
from jax.experimental import pallas as pl
from jax.experimental.pallas import tpu as pltpu
from jax.sharding import PartitionSpec as P

QH = 64
KVH = 8
HD = 128
GROUP = QH // KVH
LANES = 128
ADAPTER_SCALE = 0.5
MESH = pl.DeviceIdType.MESH
BF16 = jnp.bfloat16
F32 = jnp.float32


def stage_plan(pool, cols):
    bits = pool.bit_length() - 1
    plain = list(range(bits))
    other = [0, 2, 1] + plain[3:]
    half = cols // 2
    return [(0, half, plain), (half, cols - half, other)]


def stage_type(stage):
    return BF16 if stage < 3 else F32


def slot_of(d, order):
    bits = len(order)
    return sum(((d >> b) & 1) << (bits - 1 - j) for j, b in enumerate(order))


def kernel(pool, tensor, rd, feats, cols, rank, lmax, heads, *refs):
    bits = pool.bit_length() - 1
    plan = stage_plan(pool, cols)
    groups = len(plan)
    refs = list(refs)
    hidden, ids_ref, pages_ref, lens_ref, q_ref, w_hbm, down_hbm, up_hbm, cache_hbm = refs[:9]
    fresh_ref, att_ref = refs[9:11]
    (xs, xg, xm, w_v, down_v, up_v, kv, qs, o_acc, m_acc, l_acc, rk, rr, rs, rv) = refs[11:26]
    rest = refs[26:]
    acc = rest[:groups]
    rest = rest[groups:]
    sbuf = [[rest[(g * bits + j) * 2] for j in range(bits)] for g in range(groups)]
    rbuf = [[rest[(g * bits + j) * 2 + 1] for j in range(bits)] for g in range(groups)]
    rest = rest[2 * groups * bits:]
    lsem, kvsem, s1, r1, s2, r2, s3, r3, s4, r4 = rest

    me = lax.axis_index("pool")
    mt = lax.axis_index("tensor")
    rows = pool * rd
    copies_up = LANES // rank

    local = [
        pltpu.make_async_copy(down_hbm, down_v, lsem.at[0]),
        pltpu.make_async_copy(w_hbm, w_v, lsem.at[1]),
    ]
    ups = []
    for t in range(tensor):
        for i in range(copies_up):
            ups.append(
                pltpu.make_async_copy(
                    up_hbm.at[pl.ds(t * rank, rank)],
                    up_v.at[t, pl.ds(i * rank, rank)],
                    lsem.at[2 + t * copies_up + i],
                )
            )
    kvs = [pltpu.make_async_copy(cache_hbm.at[r], kv.at[r], kvsem.at[r]) for r in range(rd)]
    for c in local + ups + kvs:
        c.start()

    barrier = pltpu.get_barrier_semaphore()
    for to in range(tensor):
        tt = lax.rem(mt + to, tensor)

        def greet(k, carry, tt=tt):
            pl.semaphore_signal(
                barrier, inc=1, device_id={"pool": lax.rem(me + k, pool), "tensor": tt}, device_id_type=MESH
            )
            return carry

        lax.fori_loop(1 if to == 0 else 0, pool, greet, 0)

    for d in range(pool):
        xs[d] = hidden[:, d * feats:(d + 1) * feats]
    xg[me] = xs[me]
    pl.semaphore_wait(barrier, pool * tensor - 1)

    def hid_copy(k, to, slot):
        return pltpu.make_async_remote_copy(
            src_ref=xs.at[to], dst_ref=xg.at[slot], send_sem=s1.at[k], recv_sem=r1.at[k],
            device_id={"pool": to}, device_id_type=MESH,
        )

    def rank_copy(k, to, slot):
        return pltpu.make_async_remote_copy(
            src_ref=rk.at[to], dst_ref=rr.at[slot], send_sem=s2.at[k], recv_sem=r2.at[k],
            device_id={"pool": to}, device_id_type=MESH,
        )

    def vec_copy(off, k, to, tt, slot, ts):
        return pltpu.make_async_remote_copy(
            src_ref=rs, dst_ref=rv.at[ts, slot], send_sem=s3.at[off, k], recv_sem=r3.at[off, k],
            device_id={"pool": to, "tensor": tt}, device_id_type=MESH,
        )

    def each(first, fn):
        def step(k, carry):
            fn(k, lax.rem(me + k, pool), lax.rem(me + pool - k, pool))
            return carry

        lax.fori_loop(first, pool, step, 0)

    each(1, lambda k, to, frm: hid_copy(k, to, me).start())

    nq = heads * GROUP
    for j in range(nq):
        qs[pl.ds(j, rd, stride=nq), :] = q_ref[:, j * HD:(j + 1) * HD].astype(F32)
    inv_root = 1.0 / math.sqrt(HD)

    def attend(r0, r1_):
        for r in range(r0, r1_):
            kvs[r].wait()

        def row(r, carry):
            live = lax.broadcasted_iota(jnp.int32, (nq, lmax), 1) < lens_ref[r]
            q_row = qs[pl.ds(pl.multiple_of(r * nq, nq), nq), :].astype(BF16)
            parts = []
            for h in range(heads):
                k_h = kv[r, :, 2 * h * HD:(2 * h + 1) * HD]
                parts.append(
                    lax.dot_general(
                        q_row[h * GROUP:(h + 1) * GROUP], k_h, (((1,), (1,)), ((), ())),
                        preferred_element_type=F32,
                    )
                )
            s = jnp.concatenate(parts, axis=0) * inv_root
            s = jnp.where(live, s, -jnp.inf)
            m = jnp.max(s, axis=-1, keepdims=True)
            p = jnp.exp(s - m)
            l = jnp.sum(p, axis=-1, keepdims=True)
            pb = p.astype(BF16)
            outs = []
            for h in range(heads):
                v_h = kv[r, :, (2 * h + 1) * HD:(2 * h + 2) * HD]
                outs.append(
                    jnp.dot(pb[h * GROUP:(h + 1) * GROUP], v_h, preferred_element_type=F32)
                )
            at = pl.ds(pl.multiple_of(r * nq, nq), nq)
            o_acc[at, :] = jnp.concatenate(outs, axis=0)
            m_acc[at, :] = jnp.broadcast_to(m, (nq, LANES))
            l_acc[at, :] = jnp.broadcast_to(l, (nq, LANES))
            return carry

        lax.fori_loop(r0, r1_, row, 0)

    local[0].wait()
    attend(0, 2)

    each(1, lambda k, to, frm: hid_copy(k, to, frm).wait_recv())
    xm[...] = xg[...].astype(F32).reshape(rows, feats).astype(BF16)
    ids = ids_ref[...]
    total = jnp.zeros((rows, LANES), F32)
    lane_sub = lax.broadcasted_iota(jnp.int32, (rows, LANES), 1) // rank
    for c in range(down_v.shape[0] // LANES):
        y = lax.dot_general(
            xm[...], down_v[c * LANES:(c + 1) * LANES, :], (((1,), (1,)), ((), ())),
            preferred_element_type=F32,
        )
        total = total + jnp.where(lane_sub + c * copies_up == ids, y, 0.0)
    rk[...] = total.reshape(pool, rd, LANES)
    rr[me] = rk[me]
    each(1, lambda k, to, frm: rank_copy(k, to, me).start())

    attend(2, 4)

    each(1, lambda k, to, frm: rank_copy(k, to, frm).wait_recv())
    mine = jnp.sum(rr[...], axis=0).astype(BF16)
    rs[...] = mine
    rv[mt, me] = mine
    for off in range(tensor):
        tt = lax.rem(mt + off, tensor)
        each(1 if off == 0 else 0, lambda k, to, frm: vec_copy(off, k, to, tt, me, mt).start())

    attend(4, 6)

    for c in local[1:] + ups:
        c.wait()
    for off in range(tensor):
        tf = lax.rem(mt + tensor - off, tensor)
        each(1 if off == 0 else 0, lambda k, to, frm: vec_copy(off, k, to, mt, frm, tf).wait_recv())
    pages = pages_ref[...]
    my_adapter = jnp.sum(
        jnp.where(pages == me, lax.broadcasted_iota(jnp.int32, pages.shape, 1), 0), axis=1, keepdims=True
    )
    held = ids == my_adapter
    vecs = [
        jnp.where(held, rv[t].astype(F32).reshape(rows, LANES), 0.0).astype(BF16) for t in range(tensor)
    ]
    width = 256

    def piece(g, j):
        half = pool >> (j + 1)
        bit = plan[g][2][j]
        partner_bit = lax.rem(me // (1 << bit), 2)
        partner = me + (1 - 2 * partner_bit) * (1 << bit)
        copy = pltpu.make_async_remote_copy(
            src_ref=sbuf[g][j], dst_ref=rbuf[g][j], send_sem=s4.at[g, j], recv_sem=r4.at[g, j],
            device_id={"pool": partner}, device_id_type=MESH,
        )
        return half, partner_bit, copy

    offs = [0] * groups
    sent = []
    for g, (c0, cn, order) in enumerate(plan):
        for c in range(0, cn, width):
            at = slice(c0 + c, c0 + c + width)
            part = jnp.dot(xm[...], w_v[:, at], preferred_element_type=F32)
            for t in range(tensor):
                part = part + ADAPTER_SCALE * jnp.dot(vecs[t], up_v[t, :, at], preferred_element_type=F32)
            for d in range(pool):
                acc[g][slot_of(d, order), :, c:c + width] = part[d * rd:(d + 1) * rd]
        half, b, copy = piece(g, 0)
        sbuf[g][0][...] = acc[g][pl.ds((1 - b) * half, half)].astype(stage_type(0))
        copy.start()
        sent.append(copy)
        offs[g] = b * half
    cuts = {1: (6, 7), 2: (7, 8)}
    for j in range(1, bits):
        if j in cuts:
            attend(*cuts[j])
        for g in range(groups):
            piece(g, j - 1)[2].wait_recv()
            half, b, copy = piece(g, j)
            away, keep = (1 - b) * half, b * half
            sbuf[g][j][...] = (
                acc[g][pl.ds(offs[g] + away, half)] + rbuf[g][j - 1][pl.ds(away, half)].astype(F32)
            ).astype(stage_type(j))
            copy.start()
            sent.append(copy)
            acc[g][pl.ds(offs[g] + keep, half)] += rbuf[g][j - 1][pl.ds(keep, half)].astype(F32)
            offs[g] = offs[g] + keep
    for g, (c0, cn, order) in enumerate(plan):
        piece(g, bits - 1)[2].wait_recv()
        fresh_ref[:, c0:c0 + cn] = (acc[g][offs[g]] + rbuf[g][bits - 1][0].astype(F32)).astype(BF16)

    for h in range(heads):
        new_k = fresh_ref[:, 2 * h * HD:(2 * h + 1) * HD].astype(F32)
        new_v = fresh_ref[:, (2 * h + 1) * HD:(2 * h + 2) * HD].astype(F32)
        for gq in range(GROUP):
            j = h * GROUP + gq
            at = pl.ds(j, rd, stride=nq)
            own = jnp.sum(qs[at, :] * new_k, axis=-1, keepdims=True) * inv_root
            m = m_acc[at, :]
            peak = jnp.maximum(m, own)
            old_w = jnp.exp(m - peak)
            own_w = jnp.exp(own - peak)
            total_w = l_acc[at, :] * old_w + own_w
            mix = o_acc[at, :] * old_w + own_w.astype(BF16).astype(F32) * new_v
            att_ref[:, j * HD:(j + 1) * HD] = (mix / total_w).astype(BF16)

    each(1, lambda k, to, frm: hid_copy(k, to, me).wait_send())
    each(1, lambda k, to, frm: rank_copy(k, to, me).wait_send())
    for off in range(tensor):
        tt = lax.rem(mt + off, tensor)
        each(1 if off == 0 else 0, lambda k, to, frm: vec_copy(off, k, to, tt, me, mt).wait_send())
    for c in sent:
        c.wait_send()


def body(pool, tensor, hidden, kv_w, down, up, ids, pages, lens, queries, cache):
    rd, width = hidden.shape
    feats, cols = kv_w.shape
    adapters, rank, _ = down.shape
    lmax = cache.shape[1]
    heads = cols // (2 * HD)
    bits = pool.bit_length() - 1
    plan = stage_plan(pool, cols)
    dma = pltpu.SemaphoreType.DMA
    vm = pltpu.VMEM
    nq = heads * GROUP
    scratch = [
        vm((pool, rd, feats), BF16),
        vm((pool, rd, feats), BF16),
        vm((pool * rd, feats), BF16),
        vm((feats, cols), BF16),
        vm((adapters * rank, feats), BF16),
        vm((tensor, LANES, cols), BF16),
        vm((rd, lmax, cols), BF16),
        vm((rd * nq, HD), F32),
        vm((rd * nq, HD), F32),
        vm((rd * nq, LANES), F32),
        vm((rd * nq, LANES), F32),
        vm((pool, rd, LANES), F32),
        vm((pool, rd, LANES), F32),
        vm((rd, LANES), BF16),
        vm((tensor, pool, rd, LANES), BF16),
    ]
    scratch += [vm((pool, rd, cn), F32) for _, cn, _ in plan]
    for _, cn, _ in plan:
        for j in range(bits):
            scratch += [vm((pool >> (j + 1), rd, cn), stage_type(j))] * 2
    scratch += [
        dma((2 + tensor * (LANES // rank),)),
        dma((rd,)),
        dma((pool,)), dma((pool,)),
        dma((pool,)), dma((pool,)),
        dma((tensor, pool)), dma((tensor, pool)),
        dma((len(plan), bits)), dma((len(plan), bits)),
    ]
    vspec = pl.BlockSpec(memory_space=pltpu.VMEM)
    hbm = pl.BlockSpec(memory_space=pl.ANY)
    return pl.pallas_call(
        functools.partial(kernel, pool, tensor, rd, feats, cols, rank, lmax, heads),
        out_shape=(
            jax.ShapeDtypeStruct((rd, cols), BF16),
            jax.ShapeDtypeStruct((rd, queries.shape[1]), BF16),
        ),
        in_specs=[vspec, vspec, vspec, pl.BlockSpec(memory_space=pltpu.SMEM), vspec, hbm, hbm, hbm, hbm],
        out_specs=(vspec, vspec),
        scratch_shapes=scratch,
        compiler_params=pltpu.CompilerParams(
            collective_id=0, has_side_effects=True, vmem_limit_bytes=52 * 1024 * 1024
        ),
    )(
        hidden, ids, pages.reshape(1, -1), lens, queries,
        kv_w, down.reshape(adapters * rank, feats), up.reshape(up.shape[1], cols), cache,
    )


def solution(mesh):
    in_specs = (
        P(("groups", "pool"), None),
        P("pool", "tensor"),
        P("groups", "tensor", "pool"),
        P(("groups", "pool"), None, "tensor"),
        P("groups", None),
        P("groups"),
        P(("groups", "pool")),
        P(("groups", "pool"), "tensor"),
        P(("groups", "pool"), None, "tensor"),
    )
    out_specs = (P(("groups", "pool"), "tensor"), P(("groups", "pool"), "tensor"))
    fn = functools.partial(body, mesh.shape["pool"], mesh.shape["tensor"])
    return jax.shard_map(fn, mesh=mesh, in_specs=in_specs, out_specs=out_specs, check_vma=False)
```

time: 246 us -> 53.5 us (0.22)
  waiting for transfers between devices: 116 us -> 0 us
  blocking collectives: 55.6 us -> 0 us
  Pallas kernels: 0 us -> 45.2 us
  local copies, waits for them, and re-layouts: 39.3 us -> 7.37 us
  matrix products: 18.3 us -> 0 us
  between operations: 14.2 us -> 0.66 us
    reduce_scatter x1 -> x0, waiting for transfers between devices: 115 us -> none  [body(): lax.psum_scatter(jnp.dot(rows_in, key_value_weight, preferred_element_typ...]
    pallas_call x0 -> x1, Pallas kernels: none -> 45.2 us  [body(): pl.pallas_call(functools.partial(kernel, pool, tensor, rd, feats, cols, r...]
    unnamed x1 -> x0, blocking collectives: 40.1 us -> none
    dot_general x6 -> x0, matrix products: 18.3 us -> none  [the longest x1 5.7 us: attend_rows(): jnp.einsum('rkgl,rlkd->rkgd', weights_b, cache_vals, preferred_element_ty...]
    unnamed x16 -> x15, local copies, waits for them, and re-layouts: 24.6 us -> 7.37 us
    all_to_all x1 -> x0, blocking collectives: 15.5 us -> none  [body(): lax.all_to_all(hidden_input, 'pool', split_axis=1, concat_axis=0, tiled=T...]
    gather x3 -> x0, local copies, waits for them, and re-layouts: 14.7 us -> none  [the longest x1 8.58 us: body(): selected_down = jnp.take(adapter_down_weight, adapter_list, axis=0)]
  transfers between devices with their start and end apart: 2 -> 0, of which waited for: 1 -> 0; matrix products, arithmetic and copies ran while one was open for 20% -> 0% of each run, Pallas kernels for 0% -> 0%
where the time goes in v1:
time: 53.5 us; the launch traced here: 53.2 us
  Pallas kernels  45.2 us (84%)
  local copies, waits for them, and re-layouts  7.37 us (14%)
  between operations  0.66 us (1%)
    pallas_call x1, Pallas kernels, body(): pl.pallas_call(functools.partial(kernel, pool, tensor, rd, feats, cols, r...  45.2 us
    unnamed x15, local copies, waits for them, and re-layouts  7.37 us

profile of v1, /device:TPU:0, one launch (start us, length us, event | category | flops | bytes accessed | tf_op | source)
XLA Modules:
  0.0 53.2 jit_solution(13811657548384833782)
XLA Ops:
  0.6 0.8 %copy.11.refs_1_ = s32[256,1]{1,0:T(8,128)S(1)} copy(s32[256,1]{0,1:T(1,128)} %param.13) | data formatting | bytes 2048 | tf_op args[4]
  1.4 0.0 copy-start
  1.5 1.2 %copy-done = bf16[256,2048]{1,0:T(8,128)(2,1)S(1)} copy-done((bf16[256,2048]{1,0:T(8,128)(2,1)S(1)}, bf16[256,2048]{1,0:T(8,128)(2,1)}, u32[]{:S(2)}) %copy-start) | copy-done | bytes 1048600
  2.7 0.0 copy-start.1
  2.7 0.9 %copy-done.1 = bf16[1,64,2048]{2,1,0:T(8,128)(2,1)S(1)} copy-done((bf16[1,64,2048]{2,1,0:T(8,128)(2,1)S(1)}, bf16[1,64,2048]{2,1,0:T(8,128)(2,1)}, u32[]{:S(2)}) %copy-start.1) | copy-done | bytes 262168
  3.6 0.0 copy-start.2
  3.6 0.9 %copy-done.2 = bf16[8,8192]{1,0:T(8,128)(2,1)S(1)} copy-done((bf16[8,8192]{1,0:T(8,128)(2,1)S(1)}, bf16[8,8192]{1,0:T(8,128)(2,1)}, u32[]{:S(2)}) %copy-start.2) | copy-done | bytes 131096
  4.5 0.0 copy-start.3
  4.5 0.9 %copy-done.3 = bf16[8,8192]{1,0:T(8,128)(2,1)S(1)} copy-done((bf16[8,8192]{1,0:T(8,128)(2,1)S(1)}, bf16[8,8192]{1,0:T(8,128)(2,1)}, u32[]{:S(2)}) %copy-start.3) | copy-done | bytes 131096
  5.4 0.0 copy-start.4
  5.4 0.7 %copy-done.4 = s32[32]{0:T(128)S(1)} copy-done((s32[32]{0:T(128)S(1)}, s32[32]{0:T(128)}, u32[]{:S(2)}) %copy-start.4) | copy-done | bytes 152
  6.1 0.0 copy-start.5
  6.1 0.7 %copy-done.5 = s32[8]{0:T(128)S(1)} copy-done((s32[8]{0:T(128)S(1)}, s32[8]{0:T(128)}, u32[]{:S(2)}) %copy-start.5) | copy-done | bytes 56
  6.7 45.2 %shard_map.104 = (bf16[8,2048]{1,0:T(8,128)(2,1)S(1)}, bf16[8,8192]{1,0:T(8,128)(2,1)S(1)}) custom-call(bf16[8,8192]{1,0:T(8,128)(2,1)S(1)} %copy-done.2, s32[256,1]{1,0:T(8,128)S(1)} %copy.11.refs_1_, s32[1,32]{1,0:T(1,128)S(1)} %bitcast.4, s32[8]{0:T(128)S(1)} %copy-done.5, bf16[8,8192]{1,0:T(8,128)(2,1)S(1)} %copy-done.3, bf16[256,2048]{1,0:T(8,128)(2,1)S(1)} %copy-done, ...), custom_call_target="tpu_custom_call" | custom-call | tf_op jit(solution)/shard_map/pallas_call | solution.py:319
  52.0 0.6 %copy.14 = bf16[8,2048]{1,0:T(8,128)(2,1)} copy(bf16[8,2048]{1,0:T(8,128)(2,1)S(1)} %get-tuple-element.4) | data formatting | bytes 65536
  52.6 0.7 %copy.15 = bf16[8,8192]{1,0:T(8,128)(2,1)} copy(bf16[8,8192]{1,0:T(8,128)(2,1)S(1)} %get-tuple-element.5) | data formatting | bytes 262144
Async XLA Ops:
  1.4 1.2 %copy-start = (bf16[256,2048]{1,0:T(8,128)(2,1)S(1)}, bf16[256,2048]{1,0:T(8,128)(2,1)}, u32[]{:S(2)}) copy-start(bf16[256,2048]{1,0:T(8,128)(2,1)} %refs_5_.1) | copy-start | bytes 3145732
  2.7 0.9 %copy-start.1 = (bf16[1,64,2048]{2,1,0:T(8,128)(2,1)S(1)}, bf16[1,64,2048]{2,1,0:T(8,128)(2,1)}, u32[]{:S(2)}) copy-start(bf16[1,64,2048]{2,1,0:T(8,128)(2,1)} %param.12) | copy-start | bytes 786436
  3.6 0.9 %copy-start.2 = (bf16[8,8192]{1,0:T(8,128)(2,1)S(1)}, bf16[8,8192]{1,0:T(8,128)(2,1)}, u32[]{:S(2)}) copy-start(bf16[8,8192]{1,0:T(8,128)(2,1)} %refs_0_.1) | copy-start | bytes 393220
  4.5 0.9 %copy-start.3 = (bf16[8,8192]{1,0:T(8,128)(2,1)S(1)}, bf16[8,8192]{1,0:T(8,128)(2,1)}, u32[]{:S(2)}) copy-start(bf16[8,8192]{1,0:T(8,128)(2,1)} %refs_4_.1) | copy-start | bytes 393220
  5.4 0.7 %copy-start.4 = (s32[32]{0:T(128)S(1)}, s32[32]{0:T(128)}, u32[]{:S(2)}) copy-start(s32[32]{0:T(128)} %param.14) | copy-start | bytes 388
  6.1 0.7 %copy-start.5 = (s32[8]{0:T(128)S(1)}, s32[8]{0:T(128)}, u32[]{:S(2)}) copy-start(s32[8]{0:T(128)} %refs_3_.1) | copy-start | bytes 100

commit v2 on v1

v2 whole, which is shorter than its diff:
```python
import functools
import math

import jax
import jax.numpy as jnp
from jax import lax
from jax.experimental import pallas as pl
from jax.experimental.pallas import tpu as pltpu
from jax.sharding import PartitionSpec as P

QH = 64
KVH = 8
HD = 128
GROUP = QH // KVH
LANES = 128
ADAPTER_SCALE = 0.5
MESH = pl.DeviceIdType.MESH
BF16 = jnp.bfloat16
F32 = jnp.float32


def orders():
    return ((1, 2), (2, 1))


def kernel(pool, tensor, rd, feats, cols, rank, lmax, heads, *refs):
    hidden, ids_hbm, pages_hbm, lens_hbm, q_hbm, w_hbm, down_hbm, up_hbm, cache_hbm = refs[:9]
    fresh_ref, att_ref = refs[9:11]
    (xg, xm, w_v, down_v, up_v, kv, q_ref, ids_raw, pages_ref, lens_ref, ids3, qs, o_acc, m_acc, l_acc,
     rk, rr, rs, rv, base, s0, t0) = refs[11:33]
    groups = len(orders())
    gw = cols // groups
    per = 7
    bufs = [refs[33 + g * per:33 + (g + 1) * per] for g in range(groups)]
    (lsem, kvsem, usem, vsem, s1, r1, s2, r2, s3, r3, sp, rp, sx, rx, sy, ry, sz, rz) = refs[33 + groups * per:]

    me = lax.axis_index("pool")
    mt = lax.axis_index("tensor")
    rows = pool * rd
    half, quarter, eighth = pool // 2, pool // 4, pool // 8
    copies_up = LANES // rank
    hr = half * rd

    def bit_of(d, b):
        return lax.rem(d // (1 << b), 2)

    def partner_of(b):
        return me + (1 - 2 * bit_of(me, b)) * (1 << b)

    core = bit_of(me, 0)

    def slot(d):
        return lax.rem(d, 2) * half + d // 2

    barrier = pltpu.get_barrier_semaphore()
    for to in range(tensor):
        tt = lax.rem(mt + to, tensor)

        def greet(k, carry, tt=tt):
            pl.semaphore_signal(
                barrier, inc=1, device_id={"pool": lax.rem(me + k, pool), "tensor": tt}, device_id_type=MESH
            )
            return carry

        lax.fori_loop(1 if to == 0 else 0, pool, greet, 0)

    def hidden_cols(d):
        return hidden.at[:, pl.ds(pl.multiple_of(d * feats, feats), feats)]

    own_x = pltpu.make_async_copy(hidden_cols(me), xg.at[slot(me)], lsem.at[0])
    c_q = pltpu.make_async_copy(q_hbm, q_ref, lsem.at[1])
    c_ids = pltpu.make_async_copy(ids_hbm, ids_raw, lsem.at[2])
    c_pages = pltpu.make_async_copy(pages_hbm, pages_ref, lsem.at[3])
    c_lens = pltpu.make_async_copy(lens_hbm, lens_ref, lsem.at[4])
    c_down = pltpu.make_async_copy(down_hbm, down_v, lsem.at[5])
    c_w = pltpu.make_async_copy(w_hbm, w_v, lsem.at[6])
    ups = []
    pups = []
    for t in range(tensor):
        for i in range(copies_up):
            src = up_hbm.at[pl.ds(t * rank, rank)]
            n = t * copies_up + i
            ups.append(pltpu.make_async_copy(src, up_v.at[0, t, pl.ds(i * rank, rank)], usem.at[n]))
            pups.append(
                pltpu.make_async_remote_copy(
                    src_ref=src, dst_ref=up_v.at[1, t, pl.ds(i * rank, rank)],
                    send_sem=sp.at[n], recv_sem=rp.at[n],
                    device_id={"pool": partner_of(0)}, device_id_type=MESH,
                )
            )
    kvs = [pltpu.make_async_copy(cache_hbm.at[r], kv.at[r], kvsem.at[r]) for r in range(rd)]
    for c in [own_x, c_q, c_ids, c_pages, c_lens, c_down, c_w] + kvs[:2] + ups + kvs[2:]:
        c.start()

    pl.semaphore_wait(barrier, pool * tensor - 1)

    def hid_copy(k, to, at):
        return pltpu.make_async_remote_copy(
            src_ref=hidden_cols(to), dst_ref=xg.at[at], send_sem=s1.at[k], recv_sem=r1.at[k],
            device_id={"pool": to}, device_id_type=MESH,
        )

    def rank_copy(k, to, at):
        return pltpu.make_async_remote_copy(
            src_ref=rk.at[slot(to)], dst_ref=rr.at[at], send_sem=s2.at[k], recv_sem=r2.at[k],
            device_id={"pool": to}, device_id_type=MESH,
        )

    def vec_copy(off, k, to, tt, at, ts):
        return pltpu.make_async_remote_copy(
            src_ref=rs, dst_ref=rv.at[ts, at], send_sem=s3.at[off, k], recv_sem=r3.at[off, k],
            device_id={"pool": to, "tensor": tt}, device_id_type=MESH,
        )

    def each(first, fn, count=pool, stride=1):
        def step(k, carry):
            fn(k, lax.rem(me + k * stride, pool), lax.rem(me + pool - k * stride, pool))
            return carry

        lax.fori_loop(first, count, step, 0)

    each(1, lambda k, to, frm: hid_copy(k, to, slot(me)).start())
    for c in pups:
        c.start()

    nq = heads * GROUP
    c_q.wait()
    for j in range(nq):
        qs[pl.ds(j, rd, stride=nq), :] = q_ref[:, j * HD:(j + 1) * HD].astype(F32)
    inv_root = 1.0 / math.sqrt(HD)
    c_ids.wait()
    ids_t = jnp.broadcast_to(ids_raw[...], (LANES, rows)).T
    for d in range(pool):
        ids3[(d % 2) * half + d // 2] = ids_t[d * rd:(d + 1) * rd]
    c_pages.wait()
    c_lens.wait()

    def attend(r0, r1_):
        for r in range(r0, r1_):
            kvs[r].wait()

        def row(r, carry):
            live = lax.broadcasted_iota(jnp.int32, (nq, lmax), 1) < lens_ref[r]
            q_row = qs[pl.ds(pl.multiple_of(r * nq, nq), nq), :].astype(BF16)
            parts = []
            for h in range(heads):
                k_h = kv[r, :, 2 * h * HD:(2 * h + 1) * HD]
                parts.append(
                    lax.dot_general(
                        q_row[h * GROUP:(h + 1) * GROUP], k_h, (((1,), (1,)), ((), ())),
                        preferred_element_type=F32,
                    )
                )
            s = jnp.concatenate(parts, axis=0) * inv_root
            s = jnp.where(live, s, -jnp.inf)
            m = jnp.max(s, axis=-1, keepdims=True)
            p = jnp.exp(s - m)
            l = jnp.sum(p, axis=-1, keepdims=True)
            pb = p.astype(BF16)
            outs = []
            for h in range(heads):
                v_h = kv[r, :, (2 * h + 1) * HD:(2 * h + 2) * HD]
                outs.append(
                    jnp.dot(pb[h * GROUP:(h + 1) * GROUP], v_h, preferred_element_type=F32)
                )
            at = pl.ds(pl.multiple_of(r * nq, nq), nq)
            o_acc[at, :] = jnp.concatenate(outs, axis=0)
            m_acc[at, :] = jnp.broadcast_to(m, (nq, LANES))
            l_acc[at, :] = jnp.broadcast_to(l, (nq, LANES))
            return carry

        lax.fori_loop(r0, r1_, row, 0)

    c_down.wait()
    c_w.wait()
    attend(0, 2)

    own_x.wait()
    each(1, lambda k, to, frm: hid_copy(k, to, slot(frm)).wait_recv())
    xm[...] = xg[...].astype(F32).reshape(rows, feats).astype(BF16)
    ids = ids3[...].reshape(rows, LANES)
    total = jnp.zeros((rows, LANES), F32)
    lane_sub = lax.broadcasted_iota(jnp.int32, (rows, LANES), 1) // rank
    for c in range(down_v.shape[0] // LANES):
        y = lax.dot_general(
            xm[...], down_v[c * LANES:(c + 1) * LANES, :], (((1,), (1,)), ((), ())),
            preferred_element_type=F32,
        )
        total = total + jnp.where(lane_sub + c * copies_up == ids, y, 0.0)
    rk[...] = total.reshape(pool, rd, LANES).astype(BF16)
    rr[me] = rk[slot(me)]
    each(1, lambda k, to, frm: rank_copy(k, to, me).start())

    width = 256
    away_rows = xm[pl.ds(pl.multiple_of((1 - core) * hr, hr), hr), :]
    for c in range(0, cols, width):
        s0[:, c:c + width] = jnp.dot(away_rows, w_v[:, c:c + width], preferred_element_type=F32).astype(BF16)
    pair = pltpu.make_async_remote_copy(
        src_ref=s0, dst_ref=t0, send_sem=vsem.at[0], recv_sem=vsem.at[1],
        device_id={"pool": partner_of(0)}, device_id_type=MESH,
    )
    pair.start()
    kept_rows = xm[pl.ds(pl.multiple_of(core * hr, hr), hr), :]
    for c in range(0, cols, width):
        base[:, c:c + width] = jnp.dot(kept_rows, w_v[:, c:c + width], preferred_element_type=F32)

    attend(2, 4)

    each(1, lambda k, to, frm: rank_copy(k, to, frm).wait_recv())
    mine = jnp.sum(rr[...].astype(F32), axis=0).astype(BF16)
    rs[...] = mine
    rv[mt, me // 2] = mine
    for off in range(tensor):
        tt = lax.rem(mt + off, tensor)
        each(1 if off == 0 else 0, lambda k, to, frm: vec_copy(off, k, to, tt, me // 2, mt).start(), half, 2)

    attend(4, 6)

    pair.wait_recv()
    for c in ups:
        c.wait()
    for c in pups:
        c.wait_recv()
    for off in range(tensor):
        tf = lax.rem(mt + tensor - off, tensor)
        each(
            1 if off == 0 else 0,
            lambda k, to, frm: vec_copy(off, k, to, mt, frm // 2, tf).wait_recv(), half, 2,
        )
    pages = pages_ref[...]
    ids_half = ids3[pl.ds(core * half, half)].reshape(hr, LANES)
    vecs = []
    for i, holder in enumerate((me, partner_of(0))):
        adapter = jnp.sum(
            jnp.where(pages == holder, lax.broadcasted_iota(jnp.int32, pages.shape, 1), 0), axis=1, keepdims=True
        )
        for t in range(tensor):
            vec = jnp.where(ids_half == adapter, rv[t].astype(F32).reshape(hr, LANES), 0.0).astype(BF16)
            vecs.append((vec, i, t))

    def hop(g, j):
        sems = ((sx, rx), (sy, ry))[j]
        return pltpu.make_async_remote_copy(
            src_ref=bufs[g][1 + 2 * j], dst_ref=bufs[g][2 + 2 * j],
            send_sem=sems[0].at[g], recv_sem=sems[1].at[g],
            device_id={"pool": partner_of(orders()[g][j])}, device_id_type=MESH,
        )

    zi = me // 8

    def last_copy(g, k):
        to = lax.rem(zi + k, eighth)
        return pltpu.make_async_remote_copy(
            src_ref=bufs[g][5].at[to], dst_ref=bufs[g][6].at[k - 1],
            send_sem=sz.at[g, k], recv_sem=rz.at[g, k],
            device_id={"pool": lax.rem(me, 8) + 8 * to}, device_id_type=MESH,
        )

    offs = []
    for g, (b1, b2) in enumerate(orders()):
        acc, x_out = bufs[g][0], bufs[g][1]
        for c in range(0, gw, width):
            at = slice(g * gw + c, g * gw + c + width)
            part = base[:, at] + t0[:, at].astype(F32)
            for vec, i, t in vecs:
                part = part + ADAPTER_SCALE * jnp.dot(vec, up_v[i, t, :, at], preferred_element_type=F32)
            for n in range(half):
                d = 2 * n
                where = ((d >> b1) & 1) * quarter + ((d >> b2) & 1) * eighth + d // 8
                acc[where, :, c:c + width] = part[n * rd:(n + 1) * rd]
        b = bit_of(me, b1)
        x_out[...] = acc[pl.ds((1 - b) * quarter, quarter)].astype(BF16)
        hop(g, 0).start()
        offs.append(b * quarter)
    attend(6, 7)
    for g, (b1, b2) in enumerate(orders()):
        acc, _, x_in, y_out = bufs[g][:4]
        hop(g, 0).wait_recv()
        b = bit_of(me, b2)
        away, keep = (1 - b) * eighth, b * eighth
        y_out[...] = (acc[pl.ds(offs[g] + away, eighth)] + x_in[pl.ds(away, eighth)].astype(F32)).astype(BF16)
        hop(g, 1).start()
        acc[pl.ds(offs[g] + keep, eighth)] += x_in[pl.ds(keep, eighth)].astype(F32)
        offs[g] = offs[g] + keep
    attend(7, 8)
    for g in range(groups):
        acc, _, _, _, y_in, z_out, _ = bufs[g]
        hop(g, 1).wait_recv()
        full = acc[pl.ds(offs[g], eighth)] + y_in[...].astype(F32)
        acc[pl.ds(offs[g], eighth)] = full
        z_out[...] = full.astype(BF16)
        for k in range(1, eighth):
            last_copy(g, k).start()
    for g in range(groups):
        acc, z_in = bufs[g][0], bufs[g][6]
        for k in range(1, eighth):
            last_copy(g, k).wait_recv()
        done = acc[offs[g] + zi]
        for k in range(1, eighth):
            done = done + z_in[k - 1].astype(F32)
        fresh_ref[:, g * gw:(g + 1) * gw] = done.astype(BF16)

    for h in range(heads):
        new_k = fresh_ref[:, 2 * h * HD:(2 * h + 1) * HD].astype(F32)
        new_v = fresh_ref[:, (2 * h + 1) * HD:(2 * h + 2) * HD].astype(F32)
        for gq in range(GROUP):
            j = h * GROUP + gq
            at = pl.ds(j, rd, stride=nq)
            own = jnp.sum(qs[at, :] * new_k, axis=-1, keepdims=True) * inv_root
            m = m_acc[at, :]
            peak = jnp.maximum(m, own)
            old_w = jnp.exp(m - peak)
            own_w = jnp.exp(own - peak)
            total_w = l_acc[at, :] * old_w + own_w
            mix = o_acc[at, :] * old_w + own_w.astype(BF16).astype(F32) * new_v
            att_ref[:, j * HD:(j + 1) * HD] = (mix / total_w).astype(BF16)

    each(1, lambda k, to, frm: hid_copy(k, to, slot(me)).wait_send())
    for c in pups:
        c.wait_send()
    each(1, lambda k, to, frm: rank_copy(k, to, me).wait_send())
    pair.wait_send()
    for off in range(tensor):
        tt = lax.rem(mt + off, tensor)
        each(1 if off == 0 else 0, lambda k, to, frm: vec_copy(off, k, to, tt, me // 2, mt).wait_send(), half, 2)
    for g in range(groups):
        hop(g, 0).wait_send()
        hop(g, 1).wait_send()
        for k in range(1, eighth):
            last_copy(g, k).wait_send()


def body(pool, tensor, hidden, kv_w, down, up, ids, pages, lens, queries, cache):
    rd, width = hidden.shape
    feats, cols = kv_w.shape
    adapters, rank, _ = down.shape
    lmax = cache.shape[1]
    heads = cols // (2 * HD)
    dma = pltpu.SemaphoreType.DMA
    vm = pltpu.VMEM
    nq = heads * GROUP
    groups = len(orders())
    gw = cols // groups
    half, quarter, eighth = pool // 2, pool // 4, pool // 8
    nup = tensor * (LANES // rank)
    scratch = [
        vm((pool, rd, feats), BF16),
        vm((pool * rd, feats), BF16),
        vm((feats, cols), BF16),
        vm((adapters * rank, feats), BF16),
        vm((2, tensor, LANES, cols), BF16),
        vm((rd, lmax, cols), BF16),
        vm((rd, queries.shape[1]), BF16),
        vm((1, pool * rd), jnp.int32),
        vm((1, adapters), jnp.int32),
        pltpu.SMEM((rd,), jnp.int32),
        vm((pool, rd, LANES), jnp.int32),
        vm((rd * nq, HD), F32),
        vm((rd * nq, HD), F32),
        vm((rd * nq, LANES), F32),
        vm((rd * nq, LANES), F32),
        vm((pool, rd, LANES), BF16),
        vm((pool, rd, LANES), BF16),
        vm((rd, LANES), BF16),
        vm((tensor, half, rd, LANES), BF16),
        vm((half * rd, cols), F32),
        vm((half * rd, cols), BF16),
        vm((half * rd, cols), BF16),
    ]
    for _ in range(groups):
        scratch += [vm((half, rd, gw), F32)]
        scratch += [vm((quarter, rd, gw), BF16)] * 2
        scratch += [vm((eighth, rd, gw), BF16)] * 2
        scratch += [vm((eighth, rd, gw), BF16), vm((eighth - 1, rd, gw), BF16)]
    scratch += [
        dma((7,)), dma((rd,)), dma((nup,)), dma((2,)),
        dma((pool,)), dma((pool,)),
        dma((pool,)), dma((pool,)),
        dma((tensor, half)), dma((tensor, half)),
        dma((nup,)), dma((nup,)),
        dma((groups,)), dma((groups,)),
        dma((groups,)), dma((groups,)),
        dma((groups, eighth)), dma((groups, eighth)),
    ]
    vspec = pl.BlockSpec(memory_space=pltpu.VMEM)
    hbm = pl.BlockSpec(memory_space=pl.ANY)
    return pl.pallas_call(
        functools.partial(kernel, pool, tensor, rd, feats, cols, rank, lmax, heads),
        out_shape=(
            jax.ShapeDtypeStruct((rd, cols), BF16),
            jax.ShapeDtypeStruct((rd, queries.shape[1]), BF16),
        ),
        in_specs=[hbm] * 9,
        out_specs=(vspec, vspec),
        scratch_shapes=scratch,
        compiler_params=pltpu.CompilerParams(
            collective_id=0, has_side_effects=True, vmem_limit_bytes=60 * 1024 * 1024
        ),
    )(
        hidden, ids.reshape(1, -1), pages.reshape(1, -1), lens, queries,
        kv_w, down.reshape(adapters * rank, feats), up.reshape(up.shape[1], cols), cache,
    )


def solution(mesh):
    in_specs = (
        P(("groups", "pool"), None),
        P("pool", "tensor"),
        P("groups", "tensor", "pool"),
        P(("groups", "pool"), None, "tensor"),
        P("groups", None),
        P("groups"),
        P(("groups", "pool")),
        P(("groups", "pool"), "tensor"),
        P(("groups", "pool"), None, "tensor"),
    )
    out_specs = (P(("groups", "pool"), "tensor"), P(("groups", "pool"), "tensor"))
    fn = functools.partial(body, mesh.shape["pool"], mesh.shape["tensor"])
    return jax.shard_map(fn, mesh=mesh, in_specs=in_specs, out_specs=out_specs, check_vma=False)
```

time: 53.5 us -> 42.5 us (0.79)
  Pallas kernels: 45.2 us -> 38.7 us
  local copies, waits for them, and re-layouts: 7.37 us -> 2.94 us
    pallas_call x1, Pallas kernels: 45.2 us -> 38.7 us  [body(): pl.pallas_call(functools.partial(kernel, pool, tensor, rd, feats, cols, r...]
    unnamed x15 -> x2, local copies, waits for them, and re-layouts: 7.37 us -> 2.94 us
where the time goes in v2:
time: 42.5 us; the launch traced here: 42.3 us
  Pallas kernels  38.7 us (91%)
  local copies, waits for them, and re-layouts  2.94 us (7%)
  between operations  0.64 us (2%)
    pallas_call x1, Pallas kernels, body(): pl.pallas_call(functools.partial(kernel, pool, tensor, rd, feats, cols, r...  38.7 us
    unnamed x2, local copies, waits for them, and re-layouts  2.94 us

profile of v2, /device:TPU:0, one launch (start us, length us, event | category | flops | bytes accessed | tf_op | source)
XLA Modules:
  0.0 42.3 jit_solution(7998123423015945875)
XLA Ops:
  0.6 38.7 %shard_map.104 = (bf16[8,2048]{1,0:T(8,128)(2,1)}, bf16[8,8192]{1,0:T(8,128)(2,1)}) custom-call(bf16[8,8192]{1,0:T(8,128)(2,1)} %refs_0_.1, s32[1,256]{1,0:T(1,128)} %bitcast.6, s32[1,32]{1,0:T(1,128)} %bitcast.7, s32[8]{0:T(128)} %refs_3_.1, bf16[8,8192]{1,0:T(8,128)(2,1)} %refs_4_.1, bf16[256,2048]{1,0:T(8,128)(2,1)} %refs_5_.1, ...), custom_call_target="tpu_custom_call" | custom-call | tf_op jit(solution)/shard_map/pallas_call | solution.py:387
  39.3 1.4 %copy.13 = bf16[8,2048]{1,0:T(8,128)(2,1)} copy(bf16[8,2048]{1,0:T(8,128)(2,1)} %get-tuple-element.4) | data formatting | bytes 65536
  40.7 1.6 %copy.14 = bf16[8,8192]{1,0:T(8,128)(2,1)} copy(bf16[8,8192]{1,0:T(8,128)(2,1)} %get-tuple-element.5) | data formatting | bytes 262144

commit v3 on v2

--- a/solution.py
+++ b/solution.py
@@ -20,7 +20,7 @@
 
 
 def orders():
-    return ((1, 2), (2, 1))
+    return ((1, 2), (2, 1), (1, 2), (2, 1))
 
 
 def kernel(pool, tensor, rd, feats, cols, rank, lmax, heads, *refs):
@@ -89,7 +89,7 @@
                 )
             )
     kvs = [pltpu.make_async_copy(cache_hbm.at[r], kv.at[r], kvsem.at[r]) for r in range(rd)]
-    for c in [own_x, c_q, c_ids, c_pages, c_lens, c_down, c_w] + kvs[:2] + ups + kvs[2:]:
+    for c in [own_x, c_q, c_ids, c_pages, c_lens, c_down, c_w] + kvs[:2]:
         c.start()
 
     pl.semaphore_wait(barrier, pool * tensor - 1)
@@ -120,7 +120,7 @@
         lax.fori_loop(first, count, step, 0)
 
     each(1, lambda k, to, frm: hid_copy(k, to, slot(me)).start())
-    for c in pups:
+    for c in pups + ups + kvs[2:]:
         c.start()
 
     nq = heads * GROUP
@@ -204,7 +204,7 @@
     for c in range(0, cols, width):
         base[:, c:c + width] = jnp.dot(kept_rows, w_v[:, c:c + width], preferred_element_type=F32)
 
-    attend(2, 4)
+    attend(2, 5)
 
     each(1, lambda k, to, frm: rank_copy(k, to, frm).wait_recv())
     mine = jnp.sum(rr[...].astype(F32), axis=0).astype(BF16)
@@ -214,7 +214,7 @@
         tt = lax.rem(mt + off, tensor)
         each(1 if off == 0 else 0, lambda k, to, frm: vec_copy(off, k, to, tt, me // 2, mt).start(), half, 2)
 
-    attend(4, 6)
+    attend(5, 7)
 
     pair.wait_recv()
     for c in ups:
@@ -255,6 +255,22 @@
             send_sem=sz.at[g, k], recv_sem=rz.at[g, k],
             device_id={"pool": lax.rem(me, 8) + 8 * to}, device_id_type=MESH,
         )
+
+    def join(h0, h1):
+        for h in range(h0, h1):
+            new_k = fresh_ref[:, 2 * h * HD:(2 * h + 1) * HD].astype(F32)
+            new_v = fresh_ref[:, (2 * h + 1) * HD:(2 * h + 2) * HD].astype(F32)
+            for gq in range(GROUP):
+                j = h * GROUP + gq
+                at = pl.ds(j, rd, stride=nq)
+                own = jnp.sum(qs[at, :] * new_k, axis=-1, keepdims=True) * inv_root
+                m = m_acc[at, :]
+                peak = jnp.maximum(m, own)
+                old_w = jnp.exp(m - peak)
+                own_w = jnp.exp(own - peak)
+                total_w = l_acc[at, :] * old_w + own_w
+                mix = o_acc[at, :] * old_w + own_w.astype(BF16).astype(F32) * new_v
+                att_ref[:, j * HD:(j + 1) * HD] = (mix / total_w).astype(BF16)
 
     offs = []
     for g, (b1, b2) in enumerate(orders()):
@@ -272,7 +288,15 @@
         x_out[...] = acc[pl.ds((1 - b) * quarter, quarter)].astype(BF16)
         hop(g, 0).start()
         offs.append(b * quarter)
-    attend(6, 7)
+    attend(7, 8)
+    each(1, lambda k, to, frm: hid_copy(k, to, slot(me)).wait_send())
+    for c in pups:
+        c.wait_send()
+    each(1, lambda k, to, frm: rank_copy(k, to, me).wait_send())
+    pair.wait_send()
+    for off in range(tensor):
+        tt = lax.rem(mt + off, tensor)
+        each(1 if off == 0 else 0, lambda k, to, frm: vec_copy(off, k, to, tt, me // 2, mt).wait_send(), half, 2)
     for g, (b1, b2) in enumerate(orders()):
         acc, _, x_in, y_out = bufs[g][:4]
         hop(g, 0).wait_recv()
@@ -282,7 +306,6 @@
         hop(g, 1).start()
         acc[pl.ds(offs[g] + keep, eighth)] += x_in[pl.ds(keep, eighth)].astype(F32)
         offs[g] = offs[g] + keep
-    attend(7, 8)
     for g in range(groups):
         acc, _, _, _, y_in, z_out, _ = bufs[g]
         hop(g, 1).wait_recv()
@@ -299,30 +322,8 @@
         for k in range(1, eighth):
             done = done + z_in[k - 1].astype(F32)
         fresh_ref[:, g * gw:(g + 1) * gw] = done.astype(BF16)
-
-    for h in range(heads):
-        new_k = fresh_ref[:, 2 * h * HD:(2 * h + 1) * HD].astype(F32)
-        new_v = fresh_ref[:, (2 * h + 1) * HD:(2 * h + 2) * HD].astype(F32)
-        for gq in range(GROUP):
-            j = h * GROUP + gq
-            at = pl.ds(j, rd, stride=nq)
-            own = jnp.sum(qs[at, :] * new_k, axis=-1, keepdims=True) * inv_root
-            m = m_acc[at, :]
-            peak = jnp.maximum(m, own)
-            old_w = jnp.exp(m - peak)
-            own_w = jnp.exp(own - peak)
-            total_w = l_acc[at, :] * old_w + own_w
-            mix = o_acc[at, :] * old_w + own_w.astype(BF16).astype(F32) * new_v
-            att_ref[:, j * HD:(j + 1) * HD] = (mix / total_w).astype(BF16)
-
-    each(1, lambda k, to, frm: hid_copy(k, to, slot(me)).wait_send())
-    for c in pups:
-        c.wait_send()
-    each(1, lambda k, to, frm: rank_copy(k, to, me).wait_send())
-    pair.wait_send()
-    for off in range(tensor):
-        tt = lax.rem(mt + off, tensor)
-        each(1 if off == 0 else 0, lambda k, to, frm: vec_copy(off, k, to, tt, me // 2, mt).wait_send(), half, 2)
+        join(g * heads // groups, (g + 1) * heads // groups)
+
     for g in range(groups):
         hop(g, 0).wait_send()
         hop(g, 1).wait_send()

time: 42.5 us -> 41.4 us (0.974)
  Pallas kernels: 38.7 us -> 37.6 us
    pallas_call x1, Pallas kernels: 38.7 us -> 37.6 us  [body(): pl.pallas_call(functools.partial(kernel, pool, tensor, rd, feats, cols, r...]
where the time goes in v3:
time: 41.4 us; the launch traced here: 41.2 us
  Pallas kernels  37.6 us (91%)
  local copies, waits for them, and re-layouts  2.94 us (7%)
  between operations  0.64 us (2%)
    pallas_call x1, Pallas kernels, body(): pl.pallas_call(functools.partial(kernel, pool, tensor, rd, feats, cols, r...  37.6 us
    unnamed x2, local copies, waits for them, and re-layouts  2.94 us

profile of v3, /device:TPU:0, one launch (start us, length us, event | category | flops | bytes accessed | tf_op | source)
XLA Modules:
  0.0 41.2 jit_solution(8062967883809349858)
XLA Ops:
  0.6 37.6 %shard_map.104 = (bf16[8,2048]{1,0:T(8,128)(2,1)}, bf16[8,8192]{1,0:T(8,128)(2,1)}) custom-call(bf16[8,8192]{1,0:T(8,128)(2,1)} %refs_0_.1, s32[1,256]{1,0:T(1,128)} %bitcast.6, s32[1,32]{1,0:T(1,128)} %bitcast.7, s32[8]{0:T(128)} %refs_3_.1, bf16[8,8192]{1,0:T(8,128)(2,1)} %refs_4_.1, bf16[256,2048]{1,0:T(8,128)(2,1)} %refs_5_.1, ...), custom_call_target="tpu_custom_call" | custom-call | tf_op jit(solution)/shard_map/pallas_call | solution.py:388
  38.2 1.4 %copy.13 = bf16[8,2048]{1,0:T(8,128)(2,1)} copy(bf16[8,2048]{1,0:T(8,128)(2,1)} %get-tuple-element.4) | data formatting | bytes 65536
  39.6 1.6 %copy.14 = bf16[8,8192]{1,0:T(8,128)(2,1)} copy(bf16[8,8192]{1,0:T(8,128)(2,1)} %get-tuple-element.5) | data formatting | bytes 262144
